TPU v7x, 512 devices: a whole 4x8x8 slice. The times are simulated.
512 devices in a mesh: region: 16 (over y, core), tile: 32 (over x, z).
Axes of the slice: x: 4, y: 8, z: 8, core: 2. Of those that a mesh axis runs over, the one named last changes fastest.
Arguments:
- prior_pressure: float32 [64, 4, 64, 4096], P(None, None, 'region', 'tile'), may hold values from -6 to 6
- infiltration_source: float32 [64, 64, 4096], P(None, 'region', 'tile'), may hold values from -6 to 6
- soil_class: int32 [4, 64, 4096], P(None, 'region', 'tile'), may hold values from 0 to 11
- soil_k: float32 [12], replicated, may hold values from 0.02 to 0.2
- obs_index: int32 [131072], P(('region', 'tile')), may hold values from 0 to 2047
- obs_value: float32 [131072], P(('region', 'tile')), may hold values from -6 to 6
- obs_var: float32 [131072], P(('region', 'tile')), may hold values from 0.5 to 8
- obs_count: int32 [512], P(('region', 'tile')), may hold values from 1 to 256, as said below
Outputs:
- analysis: float32 [64, 4, 64, 4096], P(None, None, 'region', 'tile')
Inputs may be any that keep to these rules, and one draw needn't show every extreme that they name: `obs_count`: at least one block has all 256 slots live.
All inputs are finite; a program needn't handle non-finite values.
Results may differ from a plain program's by a relative error of at most 0.00019.
Values sent between devices are 32-bit elements; how exact they have to be, the bound alone decides.
No kernel may reach another device: no remote copies, remote signals or barrier semaphores. Data moves between devices by JAX's collectives and lax.ppermute only.
A program may use at most 64 MiB of HBM per device.

v0:
```python
import jax
import jax.numpy as jnp
from jax import lax
from jax.sharding import PartitionSpec as P

STEPS = 3
step_dt = 0.25
vert_share = 0.5


def extended(block, sides, width):
    for axis, dim in sides:
        count = lax.axis_size(axis)
        forward = [(i, i + 1) for i in range(count - 1)]
        backward = [(target, source) for source, target in forward]
        low = lax.ppermute(
            lax.slice_in_dim(block, block.shape[dim] - width, None, axis=dim), axis, forward
        )
        high = lax.ppermute(lax.slice_in_dim(block, 0, width, axis=dim), axis, backward)
        block = jnp.concatenate([low, block, high], axis=dim)
    return block


def lookup(soil_class, soil_k):
    total = jnp.zeros(soil_class.shape, jnp.float32)
    for index in range(soil_k.shape[0]):
        total = total + jnp.where(soil_class == index, soil_k[index], 0.0)
    return total


def cholesky_lower(matrix):
    order = matrix.shape[0]
    places = jnp.arange(order, dtype=jnp.int32)

    def column_step(column, lower):
        onehot = (places == column.astype(jnp.int32)).astype(matrix.dtype)
        row_now = jnp.dot(onehot, lower, precision=lax.Precision.HIGHEST)
        remain = jnp.dot(matrix, onehot, precision=lax.Precision.HIGHEST) - jnp.dot(
            lower, row_now, precision=lax.Precision.HIGHEST
        )
        pivot = jnp.sqrt(jnp.sum(remain * onehot))
        fresh = jnp.where(
            places >= column.astype(jnp.int32), remain / pivot, jnp.zeros_like(remain)
        )
        return lower + fresh[:, None] * onehot[None, :]

    return lax.fori_loop(0, order, column_step, jnp.zeros_like(matrix))


def lower_inverse(lower):
    order = lower.shape[0]
    places = jnp.arange(order, dtype=jnp.int32)

    def row_step(row, solved):
        onehot = (places == row.astype(jnp.int32)).astype(lower.dtype)
        row_now = jnp.dot(onehot, lower, precision=lax.Precision.HIGHEST)
        pivot = jnp.sum(row_now * onehot)
        fresh = (onehot - jnp.dot(row_now, solved, precision=lax.Precision.HIGHEST)) / pivot
        return solved + onehot[:, None] * fresh[None, :]

    return lax.fori_loop(0, order, row_step, jnp.zeros_like(lower))


def update(padded, bordered_permeability, push):
    cond = bordered_permeability[None] * (0.5 + jax.nn.sigmoid(padded))
    center = padded[:, :, 1:-1, 1:-1]
    kcen = cond[:, :, 1:-1, 1:-1]
    flux = jnp.zeros_like(center)
    for rows, cols in (
        (slice(2, None), slice(1, -1)),
        (slice(None, -2), slice(1, -1)),
        (slice(1, -1), slice(2, None)),
        (slice(1, -1), slice(None, -2)),
    ):
        flux = flux + 0.5 * (kcen + cond[:, :, rows, cols]) * (padded[:, :, rows, cols] - center)
    upward = vert_share * 0.5 * (kcen[:, 1:] + kcen[:, :-1]) * (center[:, 1:] - center[:, :-1])
    flux = (
        flux
        + jnp.pad(upward, ((0, 0), (0, 1), (0, 0), (0, 0)))
        - jnp.pad(upward, ((0, 0), (1, 0), (0, 0), (0, 0)))
    )
    flux = flux + jnp.pad(push[:, None], ((0, 0), (0, center.shape[1] - 1), (0, 0), (0, 0)))
    return center + step_dt * flux


def propagate_pressure(state, bordered_permeability, infiltration_source):
    padded = extended(state, (("region", 2), ("tile", 3)), 1)
    return update(padded, bordered_permeability, infiltration_source)


def shards(
    prior_pressure,
    infiltration_source,
    soil_class,
    soil_k,
    obs_index,
    obs_value,
    obs_var,
    obs_count,
):
    realization_vectors = prior_pressure.shape[0]
    depth = 1
    bordered_permeability = extended(
        lookup(soil_class, soil_k), (("region", 1), ("tile", 2)), depth
    )
    predicted_pressure = prior_pressure
    for step in range(STEPS):
        predicted_pressure = propagate_pressure(
            predicted_pressure, bordered_permeability, infiltration_source
        )
    unrolled_vector = predicted_pressure.reshape(realization_vectors, -1)
    measured_pressure = jnp.take(unrolled_vector, obs_index, axis=1)
    live = (jnp.arange(obs_index.shape[0], dtype=jnp.int32) < obs_count[0]).astype(jnp.float32)
    weight = live / jnp.sqrt(obs_var)
    hmean = jnp.mean(measured_pressure, axis=0)
    anomal = (measured_pressure - hmean) * weight
    innov = (obs_value - hmean) * weight
    gram = jnp.dot(anomal, anomal.T, precision=lax.Precision.HIGHEST)
    bvec = jnp.dot(anomal, innov, precision=lax.Precision.HIGHEST)
    eye = jnp.eye(realization_vectors, dtype=jnp.float32)
    gram, bvec = lax.psum((gram, bvec), ("region", "tile"))
    lower = cholesky_lower((realization_vectors - 1.0) * eye + gram)
    inverse = lower_inverse(lower)
    wmean = jnp.dot(
        inverse.T,
        jnp.dot(inverse, bvec, precision=lax.Precision.HIGHEST),
        precision=lax.Precision.HIGHEST,
    )
    wroot = inverse.T * jnp.sqrt(realization_vectors - 1.0)
    blending_factor = wroot + wmean[:, None]
    sample_average = jnp.mean(predicted_pressure, axis=0)
    deviation_matrix = (predicted_pressure - sample_average).reshape(realization_vectors, -1)
    propagated_vector = jnp.dot(
        blending_factor.T, deviation_matrix, precision=lax.Precision.HIGHEST
    ).reshape(predicted_pressure.shape)
    return sample_average + propagated_vector


def solution(mesh):
    return jax.shard_map(
        shards,
        mesh=mesh,
        in_specs=(
            P(None, None, "region", "tile"),
            P(None, "region", "tile"),
            P(None, "region", "tile"),
            P(),
            P(("region", "tile")),
            P(("region", "tile")),
            P(("region", "tile")),
            P(("region", "tile")),
        ),
        out_specs=P(None, None, "region", "tile"),
        check_vma=False,
    )
```

profile of v0, /device:TPU:1, one launch (start us, length us, event | category | flops | bytes accessed | tf_op | source)
XLA Modules:
  0.0 435.6 jit_solution(1766568834195470314)
XLA Ops:
  0.0 1.8 fusion.141
  1.8 8.3 %select_add_fusion.1 = f32[4,4,128]{2,1,0:T(4,128)S(1)} fusion(s32[4,4,128]{2,1,0:T(4,128)} %param.14, f32[]{:T(128)} %bitcast.11, f32[]{:T(128)} %bitcast.10, f32[]{:T(128)} %bitcast.9, f32[]{:T(128)} %bitcast.8, f32[]{:T(128)} %bitcast.7, f32[]{:T(128)} %bitcast.6, f32[]{:T(128)} %bitcast.5, f32[]{:T(128)} %bitcast.4, f32[]{:T(128)} %bitcast.3, ...), kind=kLoop, calls=%fused_computation.194 | loop fusion | flops 71680 | bytes 16432 | tf_op jit(solution)/shard_map/add | solution.py:27
  10.1 4.6 %collective-permute-start = (f32[4,1,128]{2,1,0:T(1,128)S(1)}, f32[4,1,128]{2,1,0:T(1,128)S(1)}, u32[]{:S(2)}, u32[]{:S(2)}) collective-permute-start(f32[4,1,128]{2,1,0:T(1,128)S(1)} %get-tuple-element.244), channel_id=1, source_target_pairs={{0,32},{32,64},{64,96},{96,128},{128,160},{160,192},{192,224},{224... | collective-permute-start | bytes 6152 | tf_op jit(solution)/shard_map/ppermute | solution.py:16
  14.7 5.5 %collective-permute-start.1 = (f32[4,1,128]{2,1,0:T(1,128)S(1)}, f32[4,1,128]{2,1,0:T(1,128)S(1)}, u32[]{:S(2)}, u32[]{:S(2)}) collective-permute-start(f32[4,1,128]{2,1,0:T(1,128)S(1)} %get-tuple-element.245), channel_id=1, source_target_pairs={{32,0},{64,32},{96,64},{128,96},{160,128},{192,160},{224,192},{256... | collective-permute-start | bytes 6152 | tf_op jit(solution)/shard_map/ppermute | solution.py:19
  21.4 1.9 collective-permute-start.4
  23.3 2.4 collective-permute-start.5
  26.5 2.3 collective-permute-start.2
  32.0 4.1 collective-permute-start.6
  38.8 2.6 collective-permute-done.7
  44.5 5.1 %collective-permute-start.8 = (f32[64,4,1,128]{3,0,2,1:T(8,128)S(1)}, f32[64,4,1,128]{3,0,2,1:T(8,128)S(1)}, u32[]{:S(2)}, u32[]{:S(2)}) collective-permute-start(f32[64,4,1,128]{3,0,2,1:T(8,128)S(1)} %get-tuple-element.238), channel_id=1, source_target_pairs={{0,32},{32,64},{64,96},{96,128},{128,160},{160,192},{192,224},{224... | collective-permute-start | bytes 393224 | tf_op jit(solution)/shard_map/ppermute | solution.py:16
  49.6 1.9 collective-permute-start.9
  51.5 4.3 collective-permute-done.9
  56.6 5.2 %collective-permute-start.10 = (f32[64,4,6,1]{0,1,3,2:T(4,128)S(1)}, f32[64,4,6,1]{0,1,3,2:T(4,128)S(1)}, u32[]{:S(2)}, u32[]{:S(2)}) collective-permute-start(f32[64,4,6,1]{0,1,3,2:T(4,128)S(1)} %copy.60), channel_id=1, source_target_pairs={{0,1},{1,2},{2,3},{3,4},{4,5},{5,6},{6,7},{7,8},{8,9},{9,10},{10,1... | collective-permute-start | bytes 18440 | tf_op jit(solution)/shard_map/ppermute | solution.py:16
  62.1 1.3 collective-permute-start.11
  63.7 4.3 collective-permute-done.11
  70.4 2.9 collective-permute-start.12
  73.4 1.9 collective-permute-start.13
  75.3 4.3 collective-permute-done.13
  80.3 4.9 %collective-permute-start.14 = (f32[64,4,6,1]{0,1,3,2:T(4,128)S(1)}, f32[64,4,6,1]{0,1,3,2:T(4,128)S(1)}, u32[]{:S(2)}, u32[]{:S(2)}) collective-permute-start(f32[64,4,6,1]{0,1,3,2:T(4,128)S(1)} %copy.66), channel_id=1, source_target_pairs={{0,1},{1,2},{2,3},{3,4},{4,5},{5,6},{6,7},{7,8},{8,9},{9,10},{10,1... | collective-permute-start | bytes 18440 | tf_op jit(solution)/shard_map/ppermute | solution.py:16
  85.5 1.3 collective-permute-start.15
  87.8 2.4 collective-permute-done.15
  94.9 106.0 %all-reduce.7 = (f32[64,64]{1,0:T(8,128)S(1)}, f32[64]{0:T(128)S(1)}) all-reduce(f32[64,64]{1,0:T(8,128)S(1)} %fusion.112, f32[64]{0:T(128)S(1)} %convolution_bitcast_fusion.6), channel_id=1, replica_groups=mesh['region'=16,'tile'=32] {'region','tile'}, use_global_device_ids=true, to_apply=%region_2.3 | all-reduce | flops 4160 | bytes 33280 | tf_op jit(solution)/shard_map/psum | solution.py:121
  200.9 120.4 %while.30 = (s32[]{:T(128)}, f32[64,64]{1,0:T(8,128)S(1)}, f32[64,64]{1,0:T(8,128)S(1)}, s32[]{:T(128)}, s32[]{:T(128)}) while((s32[]{:T(128)}, f32[64,64]{1,0:T(8,128)S(1)}, f32[64,64]{1,0:T(8,128)S(1)}, s32[]{:T(128)}, s32[]{:T(128)}) %tuple.90), condition=%wide.region_5.6_spmd.clone.clone, body=%wide.region_3.5_spmd.clone.clone.sunk | while | flops 168642 | bytes 84589 | solution.py:47
  321.2 111.2 %while.29 = (s32[]{:T(128)}, f32[64,64]{1,0:T(8,128)S(1)}, f32[64,64]{1,0:T(8,128)S(1)}, s32[]{:T(128)}, s32[]{:T(128)}) while((s32[]{:T(128)}, f32[64,64]{1,0:T(8,128)S(1)}, f32[64,64]{1,0:T(8,128)S(1)}, s32[]{:T(128)}, s32[]{:T(128)}) %tuple.93), condition=%wide.region_8.9_spmd.clone, body=%wide.region_6.8_spmd.clone.sunk | while | flops 115330 | bytes 67164 | solution.py:61
  (734 shorter events, 210.1 us)
Async XLA Ops:
  0.0 30.1 %copy-start = (f32[64,4,4,128]{3,2,1,0:T(4,128)S(1)}, f32[64,4,4,128]{3,2,1,0:T(4,128)}, u32[]{:S(2)}) copy-start(f32[64,4,4,128]{3,2,1,0:T(4,128)} %param.12) | copy-start | bytes 1572868
  0.0 25.8 %copy-start.7 = (f32[64,4,128]{2,1,0:T(4,128)S(1)}, f32[64,4,128]{2,1,0:T(4,128)}, u32[]{:S(2)}) copy-start(f32[64,4,128]{2,1,0:T(4,128)} %param.13) | copy-start | bytes 393220
  10.1 15.7 %collective-permute-start = (f32[4,1,128]{2,1,0:T(1,128)S(1)}, f32[4,1,128]{2,1,0:T(1,128)S(1)}, u32[]{:S(2)}, u32[]{:S(2)}) collective-permute-start(f32[4,1,128]{2,1,0:T(1,128)S(1)} %get-tuple-element.244), channel_id=1, source_target_pairs={{0,32},{32,64},{64,96},{96,128},{128,160},{160,192},{192,224},{224... | collective-permute-start | bytes 6152 | tf_op jit(solution)/shard_map/ppermute | solution.py:16
  14.7 11.1 %collective-permute-start.1 = (f32[4,1,128]{2,1,0:T(1,128)S(1)}, f32[4,1,128]{2,1,0:T(1,128)S(1)}, u32[]{:S(2)}, u32[]{:S(2)}) collective-permute-start(f32[4,1,128]{2,1,0:T(1,128)S(1)} %get-tuple-element.245), channel_id=1, source_target_pairs={{32,0},{64,32},{96,64},{128,96},{160,128},{192,160},{224,192},{256... | collective-permute-start | bytes 6152 | tf_op jit(solution)/shard_map/ppermute | solution.py:19
  21.4 8.6 %collective-permute-start.4 = (f32[64,4,1,128]{3,0,2,1:T(8,128)S(1)}, f32[64,4,1,128]{3,0,2,1:T(8,128)S(1)}, u32[]{:S(2)}, u32[]{:S(2)}) collective-permute-start(f32[64,4,1,128]{3,0,2,1:T(8,128)S(1)} %get-tuple-element.241), channel_id=1, source_target_pairs={{0,32},{32,64},{64,96},{96,128},{128,160},{160,192},{192,224},{224... | collective-permute-start | bytes 393224 | tf_op jit(solution)/shard_map/ppermute | solution.py:16
  23.3 6.9 %collective-permute-start.5 = (f32[64,4,1,128]{3,0,2,1:T(8,128)S(1)}, f32[64,4,1,128]{3,0,2,1:T(8,128)S(1)}, u32[]{:S(2)}, u32[]{:S(2)}) collective-permute-start(f32[64,4,1,128]{3,0,2,1:T(8,128)S(1)} %get-tuple-element.240), channel_id=1, source_target_pairs={{32,0},{64,32},{96,64},{128,96},{160,128},{192,160},{224,192},{256... | collective-permute-start | bytes 393224 | tf_op jit(solution)/shard_map/ppermute | solution.py:19
  26.5 11.1 %collective-permute-start.2 = (f32[4,6,1]{2,1,0:T(8,128)}, f32[4,6,1]{2,1,0:T(8,128)}, u32[]{:S(2)}, u32[]{:S(2)}) collective-permute-start(f32[4,6,1]{2,1,0:T(8,128)} %get-tuple-element.242), channel_id=1, source_target_pairs={{0,1},{1,2},{2,3},{3,4},{4,5},{5,6},{6,7},{7,8},{8,9},{9,10},{10,1... | collective-permute-start | bytes 296 | tf_op jit(solution)/shard_map/ppermute | solution.py:16
  28.8 8.9 %collective-permute-start.3 = (f32[4,6,1]{2,1,0:T(8,128)}, f32[4,6,1]{2,1,0:T(8,128)}, u32[]{:S(2)}, u32[]{:S(2)}) collective-permute-start(f32[4,6,1]{2,1,0:T(8,128)} %get-tuple-element.243), channel_id=1, source_target_pairs={{1,0},{2,1},{3,2},{4,3},{5,4},{6,5},{7,6},{8,7},{9,8},{10,9},{11,1... | collective-permute-start | bytes 296 | tf_op jit(solution)/shard_map/ppermute | solution.py:19
  32.0 6.5 %collective-permute-start.6 = (f32[64,4,6,1]{0,1,3,2:T(4,128)S(1)}, f32[64,4,6,1]{0,1,3,2:T(4,128)S(1)}, u32[]{:S(2)}, u32[]{:S(2)}) collective-permute-start(f32[64,4,6,1]{0,1,3,2:T(4,128)S(1)} %copy.44), channel_id=1, source_target_pairs={{0,1},{1,2},{2,3},{3,4},{4,5},{5,6},{6,7},{7,8},{8,9},{9,10},{10,1... | collective-permute-start | bytes 18440 | tf_op jit(solution)/shard_map/ppermute | solution.py:16
  36.3 5.1 %collective-permute-start.7 = (f32[64,4,6,1]{0,1,3,2:T(4,128)S(1)}, f32[64,4,6,1]{0,1,3,2:T(4,128)S(1)}, u32[]{:S(2)}, u32[]{:S(2)}) collective-permute-start(f32[64,4,6,1]{0,1,3,2:T(4,128)S(1)} %copy.45), channel_id=1, source_target_pairs={{1,0},{2,1},{3,2},{4,3},{5,4},{6,5},{7,6},{8,7},{9,8},{10,9},{11,1... | collective-permute-start | bytes 18440 | tf_op jit(solution)/shard_map/ppermute | solution.py:19
  38.5 4.0 copy-start.1
  42.5 1.0 copy-start.6
  44.5 7.0 %collective-permute-start.8 = (f32[64,4,1,128]{3,0,2,1:T(8,128)S(1)}, f32[64,4,1,128]{3,0,2,1:T(8,128)S(1)}, u32[]{:S(2)}, u32[]{:S(2)}) collective-permute-start(f32[64,4,1,128]{3,0,2,1:T(8,128)S(1)} %get-tuple-element.238), channel_id=1, source_target_pairs={{0,32},{32,64},{64,96},{96,128},{128,160},{160,192},{192,224},{224... | collective-permute-start | bytes 393224 | tf_op jit(solution)/shard_map/ppermute | solution.py:16
  49.6 6.3 %collective-permute-start.9 = (f32[64,4,1,128]{3,0,2,1:T(8,128)S(1)}, f32[64,4,1,128]{3,0,2,1:T(8,128)S(1)}, u32[]{:S(2)}, u32[]{:S(2)}) collective-permute-start(f32[64,4,1,128]{3,0,2,1:T(8,128)S(1)} %get-tuple-element.239), channel_id=1, source_target_pairs={{32,0},{64,32},{96,64},{128,96},{160,128},{192,160},{224,192},{256... | collective-permute-start | bytes 393224 | tf_op jit(solution)/shard_map/ppermute | solution.py:19
  56.3 7.1 %copy-start.8 = (s32[256]{0:T(256)S(1)}, s32[256]{0:T(256)}, u32[]{:S(2)}) copy-start(s32[256]{0:T(256)} %param.16) | copy-start | bytes 3076
  56.3 12.1 %copy-start.2 = (f32[4,6,130]{2,1,0:T(8,128)S(1)}, f32[4,6,130]{2,1,0:T(8,128)}, u32[]{:S(2)}) copy-start(f32[4,6,130]{2,1,0:T(8,128)} %copy-done.1) | copy-start | bytes 37444
  56.6 6.8 %collective-permute-start.10 = (f32[64,4,6,1]{0,1,3,2:T(4,128)S(1)}, f32[64,4,6,1]{0,1,3,2:T(4,128)S(1)}, u32[]{:S(2)}, u32[]{:S(2)}) collective-permute-start(f32[64,4,6,1]{0,1,3,2:T(4,128)S(1)} %copy.60), channel_id=1, source_target_pairs={{0,1},{1,2},{2,3},{3,4},{4,5},{5,6},{6,7},{7,8},{8,9},{9,10},{10,1... | collective-permute-start | bytes 18440 | tf_op jit(solution)/shard_map/ppermute | solution.py:16
  62.1 5.9 %collective-permute-start.11 = (f32[64,4,6,1]{0,1,3,2:T(4,128)S(1)}, f32[64,4,6,1]{0,1,3,2:T(4,128)S(1)}, u32[]{:S(2)}, u32[]{:S(2)}) collective-permute-start(f32[64,4,6,1]{0,1,3,2:T(4,128)S(1)} %copy.61), channel_id=1, source_target_pairs={{1,0},{2,1},{3,2},{4,3},{5,4},{6,5},{7,6},{8,7},{9,8},{10,9},{11,1... | collective-permute-start | bytes 18440 | tf_op jit(solution)/shard_map/ppermute | solution.py:19
  70.4 4.9 %collective-permute-start.12 = (f32[64,4,1,128]{3,0,2,1:T(8,128)S(1)}, f32[64,4,1,128]{3,0,2,1:T(8,128)S(1)}, u32[]{:S(2)}, u32[]{:S(2)}) collective-permute-start(f32[64,4,1,128]{3,0,2,1:T(8,128)S(1)} %get-tuple-element.236), channel_id=1, source_target_pairs={{0,32},{32,64},{64,96},{96,128},{128,160},{160,192},{192,224},{224... | collective-permute-start | bytes 393224 | tf_op jit(solution)/shard_map/ppermute | solution.py:16
  73.4 6.3 %collective-permute-start.13 = (f32[64,4,1,128]{3,0,2,1:T(8,128)S(1)}, f32[64,4,1,128]{3,0,2,1:T(8,128)S(1)}, u32[]{:S(2)}, u32[]{:S(2)}) collective-permute-start(f32[64,4,1,128]{3,0,2,1:T(8,128)S(1)} %get-tuple-element.237), channel_id=1, source_target_pairs={{32,0},{64,32},{96,64},{128,96},{160,128},{192,160},{224,192},{256... | collective-permute-start | bytes 393224 | tf_op jit(solution)/shard_map/ppermute | solution.py:19
  80.3 7.1 %collective-permute-start.14 = (f32[64,4,6,1]{0,1,3,2:T(4,128)S(1)}, f32[64,4,6,1]{0,1,3,2:T(4,128)S(1)}, u32[]{:S(2)}, u32[]{:S(2)}) collective-permute-start(f32[64,4,6,1]{0,1,3,2:T(4,128)S(1)} %copy.66), channel_id=1, source_target_pairs={{0,1},{1,2},{2,3},{3,4},{4,5},{5,6},{6,7},{7,8},{8,9},{9,10},{10,1... | collective-permute-start | bytes 18440 | tf_op jit(solution)/shard_map/ppermute | solution.py:16
  85.5 4.7 %collective-permute-start.15 = (f32[64,4,6,1]{0,1,3,2:T(4,128)S(1)}, f32[64,4,6,1]{0,1,3,2:T(4,128)S(1)}, u32[]{:S(2)}, u32[]{:S(2)}) collective-permute-start(f32[64,4,6,1]{0,1,3,2:T(4,128)S(1)} %copy.67), channel_id=1, source_target_pairs={{1,0},{2,1},{3,2},{4,3},{5,4},{6,5},{7,6},{8,7},{9,8},{10,9},{11,1... | collective-permute-start | bytes 18440 | tf_op jit(solution)/shard_map/ppermute | solution.py:19
  92.6 1.3 copy-start.9
  92.6 1.3 copy-start.10
  (3 other events, 2.2 us)
where the time goes:
time: 441 us; the launch traced here: 436 us
  matrix products  178 us (40%)
  blocking collectives  106 us (24%)
  starting transfers between devices  47.8 us (11%)
  loops' own time  45.1 us (10%)
  other arithmetic  26.4 us (6%)
  waiting for transfers between devices  18 us (4%)
  local copies, waits for them, and re-layouts  13.4 us (3%)
    psum x1, blocking collectives, shards(): gram, bvec = lax.psum((gram, bvec), ('region', 'tile'))  106 us
    dot_general x64, matrix products, column_step(): jnp.dot(lower, row_now, precision=lax.Precision.HIGHEST)  53.6 us
    dot_general x64, matrix products, row_step(): row_now = jnp.dot(onehot, lower, precision=lax.Precision.HIGHEST)  52.8 us
    dot_general x64, matrix products, row_step(): jnp.dot(row_now, solved, precision=lax.Precision.HIGHEST)  52.7 us
    another operation x1, loops' own time, cholesky_lower(): return lax.fori_loop(0, order, column_step, jnp.zeros_like(matrix))  44.6 us
    ppermute x8, starting transfers between devices, extended(): lax.ppermute(lax.slice_in_dim(block, block.shape[dim] - width, None, axis...  30.9 us
    ppermute x8, waiting for transfers between devices, extended(): lax.ppermute(lax.slice_in_dim(block, 0, width, axis=dim), axis, backward)  17.9 us
    ppermute x8, starting transfers between devices, extended(): lax.ppermute(lax.slice_in_dim(block, 0, width, axis=dim), axis, backward)  16.9 us
  transfers between devices with their start and end apart: 16, of which 5 were waited for; matrix products, arithmetic and copies ran while one was open for 1% of the time, Pallas kernels for 0%

commit v1 on v0

--- a/solution.py
+++ b/solution.py
@@ -118,7 +118,7 @@
     gram = jnp.dot(anomal, anomal.T, precision=lax.Precision.HIGHEST)
     bvec = jnp.dot(anomal, innov, precision=lax.Precision.HIGHEST)
     eye = jnp.eye(realization_vectors, dtype=jnp.float32)
-    gram, bvec = lax.psum((gram, bvec), ("region", "tile"))
+    gram, bvec = lax.psum(lax.psum((gram, bvec), "tile"), "region")
     lower = cholesky_lower((realization_vectors - 1.0) * eye + gram)
     inverse = lower_inverse(lower)
     wmean = jnp.dot(

time: 441 us -> 513 us (1.16)
  blocking collectives: 106 us -> 184 us
  matrix products: 178 us -> 168 us
    psum x1 -> x2, blocking collectives: 106 us -> 184 us  [shards(): gram, bvec = lax.psum(lax.psum((gram, bvec), 'tile'), 'region')]
    dot_general x64, matrix products: 52.7 us -> 45.2 us  [row_step(): jnp.dot(row_now, solved, precision=lax.Precision.HIGHEST)]
where the time goes in v1:
time: 513 us; the launch traced here: 506 us
  blocking collectives  184 us (36%)
  matrix products  168 us (33%)
  starting transfers between devices  47.8 us (9%)
  loops' own time  47.6 us (9%)
  other arithmetic  26.4 us (5%)
  waiting for transfers between devices  18 us (4%)
  local copies, waits for them, and re-layouts  13.4 us (3%)
    psum x2, blocking collectives, shards(): gram, bvec = lax.psum(lax.psum((gram, bvec), 'tile'), 'region')  184 us
    dot_general x64, matrix products, column_step(): jnp.dot(lower, row_now, precision=lax.Precision.HIGHEST)  56.3 us
    dot_general x64, matrix products, row_step(): row_now = jnp.dot(onehot, lower, precision=lax.Precision.HIGHEST)  47.9 us
    another operation x1, loops' own time, cholesky_lower(): return lax.fori_loop(0, order, column_step, jnp.zeros_like(matrix))  47.2 us
    dot_general x64, matrix products, row_step(): jnp.dot(row_now, solved, precision=lax.Precision.HIGHEST)  45.2 us
    ppermute x8, starting transfers between devices, extended(): lax.ppermute(lax.slice_in_dim(block, block.shape[dim] - width, None, axis...  30.9 us
    ppermute x8, waiting for transfers between devices, extended(): lax.ppermute(lax.slice_in_dim(block, 0, width, axis=dim), axis, backward)  17.9 us
    ppermute x8, starting transfers between devices, extended(): lax.ppermute(lax.slice_in_dim(block, 0, width, axis=dim), axis, backward)  16.9 us
  transfers between devices with their start and end apart: 16, of which 5 were waited for; matrix products, arithmetic and copies ran while one was open for 1% of the time, Pallas kernels for 0%

profile of v1, /device:TPU:1, one launch (start us, length us, event | category | flops | bytes accessed | tf_op | source)
XLA Modules:
  0.0 506.3 jit_solution(924067659822047134)
XLA Ops:
  0.0 1.8 fusion.141
  1.8 8.3 %select_add_fusion.1 = f32[4,4,128]{2,1,0:T(4,128)S(1)} fusion(s32[4,4,128]{2,1,0:T(4,128)} %param.14, f32[]{:T(128)} %bitcast.11, f32[]{:T(128)} %bitcast.10, f32[]{:T(128)} %bitcast.9, f32[]{:T(128)} %bitcast.8, f32[]{:T(128)} %bitcast.7, f32[]{:T(128)} %bitcast.6, f32[]{:T(128)} %bitcast.5, f32[]{:T(128)} %bitcast.4, f32[]{:T(128)} %bitcast.3, ...), kind=kLoop, calls=%fused_computation.194 | loop fusion | flops 71680 | bytes 16432 | tf_op jit(solution)/shard_map/add | solution.py:27
  10.1 4.6 collective-permute-start
  14.7 5.5 %collective-permute-start.1 = (f32[4,1,128]{2,1,0:T(1,128)S(1)}, f32[4,1,128]{2,1,0:T(1,128)S(1)}, u32[]{:S(2)}, u32[]{:S(2)}) collective-permute-start(f32[4,1,128]{2,1,0:T(1,128)S(1)} %get-tuple-element.247), channel_id=1, source_target_pairs={{32,0},{64,32},{96,64},{128,96},{160,128},{192,160},{224,192},{256... | collective-permute-start | bytes 6152 | tf_op jit(solution)/shard_map/ppermute | solution.py:19
  21.4 1.9 collective-permute-start.4
  23.3 2.4 collective-permute-start.5
  26.5 2.3 collective-permute-start.2
  32.0 4.1 collective-permute-start.6
  36.3 1.3 collective-permute-start.7
  38.8 2.6 collective-permute-done.7
  44.5 5.1 %collective-permute-start.8 = (f32[64,4,1,128]{3,0,2,1:T(8,128)S(1)}, f32[64,4,1,128]{3,0,2,1:T(8,128)S(1)}, u32[]{:S(2)}, u32[]{:S(2)}) collective-permute-start(f32[64,4,1,128]{3,0,2,1:T(8,128)S(1)} %get-tuple-element.240), channel_id=1, source_target_pairs={{0,32},{32,64},{64,96},{96,128},{128,160},{160,192},{192,224},{224... | collective-permute-start | bytes 393224 | tf_op jit(solution)/shard_map/ppermute | solution.py:16
  49.6 1.9 collective-permute-start.9
  51.5 4.3 collective-permute-done.9
  56.6 5.2 %collective-permute-start.10 = (f32[64,4,6,1]{0,1,3,2:T(4,128)S(1)}, f32[64,4,6,1]{0,1,3,2:T(4,128)S(1)}, u32[]{:S(2)}, u32[]{:S(2)}) collective-permute-start(f32[64,4,6,1]{0,1,3,2:T(4,128)S(1)} %copy.60), channel_id=1, source_target_pairs={{0,1},{1,2},{2,3},{3,4},{4,5},{5,6},{6,7},{7,8},{8,9},{9,10},{10,1... | collective-permute-start | bytes 18440 | tf_op jit(solution)/shard_map/ppermute | solution.py:16
  63.7 4.3 collective-permute-done.11
  70.4 2.9 collective-permute-start.12
  73.4 1.9 collective-permute-start.13
  75.3 4.3 collective-permute-done.13
  80.3 4.9 collective-permute-start.14
  87.8 2.4 collective-permute-done.15
  94.9 112.0 %all-reduce.7 = (f32[64,64]{1,0:T(8,128)S(1)}, f32[64]{0:T(128)S(1)}) all-reduce(f32[64,64]{1,0:T(8,128)S(1)} %fusion.112, f32[64]{0:T(128)S(1)} %convolution_bitcast_fusion.6), channel_id=1, replica_groups=mesh['region'=16,'tile'=32] {'tile'}, use_global_device_ids=true, to_apply=%region_2.3 | all-reduce | flops 4160 | bytes 33280 | tf_op jit(solution)/shard_map/psum | solution.py:121
  206.9 71.8 %all-reduce.8 = (f32[64,64]{1,0:T(8,128)S(1)}, f32[64]{0:T(128)S(1)}) all-reduce(f32[64,64]{1,0:T(8,128)S(1)} %get-tuple-element.220, f32[64]{0:T(128)S(1)} %get-tuple-element.221), channel_id=1, replica_groups=mesh['region'=16,'tile'=32] {'region'}, use_global_device_ids=true, to_apply=%region_3.4 | all-reduce | flops 4160 | bytes 33280 | tf_op jit(solution)/shard_map/psum | solution.py:121
  278.7 125.6 %while.30 = (s32[]{:T(128)}, f32[64,64]{1,0:T(8,128)S(1)}, f32[64,64]{1,0:T(8,128)S(1)}, s32[]{:T(128)}, s32[]{:T(128)}) while((s32[]{:T(128)}, f32[64,64]{1,0:T(8,128)S(1)}, f32[64,64]{1,0:T(8,128)S(1)}, s32[]{:T(128)}, s32[]{:T(128)}) %tuple.90), condition=%wide.region_6.7_spmd.clone.clone, body=%wide.region_4.6_spmd.clone.clone.sunk | while | flops 168642 | bytes 84589 | solution.py:47
  404.3 98.8 %while.29 = (s32[]{:T(128)}, f32[64,64]{1,0:T(8,128)S(1)}, f32[64,64]{1,0:T(8,128)S(1)}, s32[]{:T(128)}, s32[]{:T(128)}) while((s32[]{:T(128)}, f32[64,64]{1,0:T(8,128)S(1)}, f32[64,64]{1,0:T(8,128)S(1)}, s32[]{:T(128)}, s32[]{:T(128)}) %tuple.93), condition=%wide.region_9.10_spmd.clone, body=%wide.region_7.9_spmd.clone.sunk | while | flops 115330 | bytes 67164 | solution.py:61
  (735 shorter events, 201.6 us)
Async XLA Ops:
  0.0 30.1 %copy-start = (f32[64,4,4,128]{3,2,1,0:T(4,128)S(1)}, f32[64,4,4,128]{3,2,1,0:T(4,128)}, u32[]{:S(2)}) copy-start(f32[64,4,4,128]{3,2,1,0:T(4,128)} %param.12) | copy-start | bytes 1572868
  0.0 25.8 %copy-start.7 = (f32[64,4,128]{2,1,0:T(4,128)S(1)}, f32[64,4,128]{2,1,0:T(4,128)}, u32[]{:S(2)}) copy-start(f32[64,4,128]{2,1,0:T(4,128)} %param.13) | copy-start | bytes 393220
  10.1 15.7 %collective-permute-start = (f32[4,1,128]{2,1,0:T(1,128)S(1)}, f32[4,1,128]{2,1,0:T(1,128)S(1)}, u32[]{:S(2)}, u32[]{:S(2)}) collective-permute-start(f32[4,1,128]{2,1,0:T(1,128)S(1)} %get-tuple-element.246), channel_id=1, source_target_pairs={{0,32},{32,64},{64,96},{96,128},{128,160},{160,192},{192,224},{224... | collective-permute-start | bytes 6152 | tf_op jit(solution)/shard_map/ppermute | solution.py:16
  14.7 11.1 %collective-permute-start.1 = (f32[4,1,128]{2,1,0:T(1,128)S(1)}, f32[4,1,128]{2,1,0:T(1,128)S(1)}, u32[]{:S(2)}, u32[]{:S(2)}) collective-permute-start(f32[4,1,128]{2,1,0:T(1,128)S(1)} %get-tuple-element.247), channel_id=1, source_target_pairs={{32,0},{64,32},{96,64},{128,96},{160,128},{192,160},{224,192},{256... | collective-permute-start | bytes 6152 | tf_op jit(solution)/shard_map/ppermute | solution.py:19
  21.4 8.6 %collective-permute-start.4 = (f32[64,4,1,128]{3,0,2,1:T(8,128)S(1)}, f32[64,4,1,128]{3,0,2,1:T(8,128)S(1)}, u32[]{:S(2)}, u32[]{:S(2)}) collective-permute-start(f32[64,4,1,128]{3,0,2,1:T(8,128)S(1)} %get-tuple-element.243), channel_id=1, source_target_pairs={{0,32},{32,64},{64,96},{96,128},{128,160},{160,192},{192,224},{224... | collective-permute-start | bytes 393224 | tf_op jit(solution)/shard_map/ppermute | solution.py:16
  23.3 6.9 %collective-permute-start.5 = (f32[64,4,1,128]{3,0,2,1:T(8,128)S(1)}, f32[64,4,1,128]{3,0,2,1:T(8,128)S(1)}, u32[]{:S(2)}, u32[]{:S(2)}) collective-permute-start(f32[64,4,1,128]{3,0,2,1:T(8,128)S(1)} %get-tuple-element.242), channel_id=1, source_target_pairs={{32,0},{64,32},{96,64},{128,96},{160,128},{192,160},{224,192},{256... | collective-permute-start | bytes 393224 | tf_op jit(solution)/shard_map/ppermute | solution.py:19
  26.5 11.1 %collective-permute-start.2 = (f32[4,6,1]{2,1,0:T(8,128)}, f32[4,6,1]{2,1,0:T(8,128)}, u32[]{:S(2)}, u32[]{:S(2)}) collective-permute-start(f32[4,6,1]{2,1,0:T(8,128)} %get-tuple-element.244), channel_id=1, source_target_pairs={{0,1},{1,2},{2,3},{3,4},{4,5},{5,6},{6,7},{7,8},{8,9},{9,10},{10,1... | collective-permute-start | bytes 296 | tf_op jit(solution)/shard_map/ppermute | solution.py:16
  28.8 8.9 %collective-permute-start.3 = (f32[4,6,1]{2,1,0:T(8,128)}, f32[4,6,1]{2,1,0:T(8,128)}, u32[]{:S(2)}, u32[]{:S(2)}) collective-permute-start(f32[4,6,1]{2,1,0:T(8,128)} %get-tuple-element.245), channel_id=1, source_target_pairs={{1,0},{2,1},{3,2},{4,3},{5,4},{6,5},{7,6},{8,7},{9,8},{10,9},{11,1... | collective-permute-start | bytes 296 | tf_op jit(solution)/shard_map/ppermute | solution.py:19
  32.0 6.5 %collective-permute-start.6 = (f32[64,4,6,1]{0,1,3,2:T(4,128)S(1)}, f32[64,4,6,1]{0,1,3,2:T(4,128)S(1)}, u32[]{:S(2)}, u32[]{:S(2)}) collective-permute-start(f32[64,4,6,1]{0,1,3,2:T(4,128)S(1)} %copy.44), channel_id=1, source_target_pairs={{0,1},{1,2},{2,3},{3,4},{4,5},{5,6},{6,7},{7,8},{8,9},{9,10},{10,1... | collective-permute-start | bytes 18440 | tf_op jit(solution)/shard_map/ppermute | solution.py:16
  36.3 5.1 %collective-permute-start.7 = (f32[64,4,6,1]{0,1,3,2:T(4,128)S(1)}, f32[64,4,6,1]{0,1,3,2:T(4,128)S(1)}, u32[]{:S(2)}, u32[]{:S(2)}) collective-permute-start(f32[64,4,6,1]{0,1,3,2:T(4,128)S(1)} %copy.45), channel_id=1, source_target_pairs={{1,0},{2,1},{3,2},{4,3},{5,4},{6,5},{7,6},{8,7},{9,8},{10,9},{11,1... | collective-permute-start | bytes 18440 | tf_op jit(solution)/shard_map/ppermute | solution.py:19
  38.5 4.0 copy-start.1
  42.5 1.0 copy-start.6
  44.5 7.0 %collective-permute-start.8 = (f32[64,4,1,128]{3,0,2,1:T(8,128)S(1)}, f32[64,4,1,128]{3,0,2,1:T(8,128)S(1)}, u32[]{:S(2)}, u32[]{:S(2)}) collective-permute-start(f32[64,4,1,128]{3,0,2,1:T(8,128)S(1)} %get-tuple-element.240), channel_id=1, source_target_pairs={{0,32},{32,64},{64,96},{96,128},{128,160},{160,192},{192,224},{224... | collective-permute-start | bytes 393224 | tf_op jit(solution)/shard_map/ppermute | solution.py:16
  49.6 6.3 %collective-permute-start.9 = (f32[64,4,1,128]{3,0,2,1:T(8,128)S(1)}, f32[64,4,1,128]{3,0,2,1:T(8,128)S(1)}, u32[]{:S(2)}, u32[]{:S(2)}) collective-permute-start(f32[64,4,1,128]{3,0,2,1:T(8,128)S(1)} %get-tuple-element.241), channel_id=1, source_target_pairs={{32,0},{64,32},{96,64},{128,96},{160,128},{192,160},{224,192},{256... | collective-permute-start | bytes 393224 | tf_op jit(solution)/shard_map/ppermute | solution.py:19
  56.2 7.1 %copy-start.8 = (s32[256]{0:T(256)S(1)}, s32[256]{0:T(256)}, u32[]{:S(2)}) copy-start(s32[256]{0:T(256)} %param.16) | copy-start | bytes 3076
  56.3 12.1 %copy-start.2 = (f32[4,6,130]{2,1,0:T(8,128)S(1)}, f32[4,6,130]{2,1,0:T(8,128)}, u32[]{:S(2)}) copy-start(f32[4,6,130]{2,1,0:T(8,128)} %copy-done.1) | copy-start | bytes 37444
  56.6 6.8 %collective-permute-start.10 = (f32[64,4,6,1]{0,1,3,2:T(4,128)S(1)}, f32[64,4,6,1]{0,1,3,2:T(4,128)S(1)}, u32[]{:S(2)}, u32[]{:S(2)}) collective-permute-start(f32[64,4,6,1]{0,1,3,2:T(4,128)S(1)} %copy.60), channel_id=1, source_target_pairs={{0,1},{1,2},{2,3},{3,4},{4,5},{5,6},{6,7},{7,8},{8,9},{9,10},{10,1... | collective-permute-start | bytes 18440 | tf_op jit(solution)/shard_map/ppermute | solution.py:16
  62.1 5.9 %collective-permute-start.11 = (f32[64,4,6,1]{0,1,3,2:T(4,128)S(1)}, f32[64,4,6,1]{0,1,3,2:T(4,128)S(1)}, u32[]{:S(2)}, u32[]{:S(2)}) collective-permute-start(f32[64,4,6,1]{0,1,3,2:T(4,128)S(1)} %copy.61), channel_id=1, source_target_pairs={{1,0},{2,1},{3,2},{4,3},{5,4},{6,5},{7,6},{8,7},{9,8},{10,9},{11,1... | collective-permute-start | bytes 18440 | tf_op jit(solution)/shard_map/ppermute | solution.py:19
  70.4 4.9 collective-permute-start.12
  73.4 6.3 %collective-permute-start.13 = (f32[64,4,1,128]{3,0,2,1:T(8,128)S(1)}, f32[64,4,1,128]{3,0,2,1:T(8,128)S(1)}, u32[]{:S(2)}, u32[]{:S(2)}) collective-permute-start(f32[64,4,1,128]{3,0,2,1:T(8,128)S(1)} %get-tuple-element.239), channel_id=1, source_target_pairs={{32,0},{64,32},{96,64},{128,96},{160,128},{192,160},{224,192},{256... | collective-permute-start | bytes 393224 | tf_op jit(solution)/shard_map/ppermute | solution.py:19
  80.3 7.1 %collective-permute-start.14 = (f32[64,4,6,1]{0,1,3,2:T(4,128)S(1)}, f32[64,4,6,1]{0,1,3,2:T(4,128)S(1)}, u32[]{:S(2)}, u32[]{:S(2)}) collective-permute-start(f32[64,4,6,1]{0,1,3,2:T(4,128)S(1)} %copy.66), channel_id=1, source_target_pairs={{0,1},{1,2},{2,3},{3,4},{4,5},{5,6},{6,7},{7,8},{8,9},{9,10},{10,1... | collective-permute-start | bytes 18440 | tf_op jit(solution)/shard_map/ppermute | solution.py:16
  85.5 4.7 collective-permute-start.15
  92.6 1.3 copy-start.9
  92.6 1.3 copy-start.10
  (3 other events, 2.2 us)
